TPU v7x, 32 devices: a whole 2x2x4 slice. The times are simulated.
32 devices in a mesh: groups: 2 (over y), dp: 4 (over x, core), tensor: 4 (over z).
Axes of the slice: x: 2, y: 2, z: 4, core: 2. Of those that a mesh axis runs over, the one named last changes fastest.
Arguments:
- attn_out: bfloat16 [4096, 8192], P(('groups', 'dp'), 'tensor'), parts along dimension 0, may hold values from -0.75 to 0.75
- out_grad: bfloat16 [4096, 8192], P(('groups', 'dp'), 'tensor'), parts along dimension 0, may hold values from -6 to 6
- base_weight: bfloat16 [8192, 8192], P('tensor', 'dp'), may hold values from -0.0625 to 0.0625
- delta_values: bfloat16 [128, 128, 128], P('tensor'), may hold values from -0.1796875 to 0.1796875
- block_rows: int32 [128], P('tensor'), may hold values from 0 to 63, as said below
- block_cols: int32 [128], P('tensor'), may hold values from 0 to 63
- block_owner: int32 [128], P('tensor'), may hold values from 0 to 3, as said below
Outputs:
- in_grad: bfloat16 [4096, 8192], P(('groups', 'dp'), 'tensor'), parts along dimension 0
- delta_grad: float32 [8, 32, 128, 128], P(('groups', 'tensor'), 'dp'), parts along dimension 0
There are 2 independent parts, one for each index of `groups`. A program takes and returns all parts, laid end to end along the dimension named above; an argument that names none is the same for every part. Nothing has to cross between parts.
Inputs may be any that keep to these rules, and one draw needn't show every extreme that they name: `block_rows`: piece k (entries k * 32 to k * 32 + 31) names block rows k * 16 to (k + 1) * 16 - 1; no two entries name the same block. `block_owner`: in every piece of 32 entries no owner appears more than 8 times, and some owner exactly 8 times.
All inputs are finite; a program needn't handle non-finite values.
Results may differ from a plain program's by a relative error of at most 0.0032.
Values may be sent and summed in bfloat16 or wider, within the bound.
A program may use at most 192 MiB of HBM per device.

v0:
```python
import jax
import jax.numpy as jnp
from jax import lax
from jax.sharding import PartitionSpec as P

D = 8192
BS = 128


def per_device(attn_out, out_grad, base_weight, delta_values, block_rows, block_cols, block_owner):
    tok_rows = attn_out.shape[0]
    feat_dev = attn_out.shape[1]
    row_span = feat_dev // BS
    col_span = base_weight.shape[1] // BS
    all_cols = D // BS
    dp_count = lax.axis_size("dp")
    dp_index = lax.axis_index("dp")
    piece_len = block_owner.shape[0]
    slot_cap = max(2, (piece_len + dp_count - 1) // dp_count)
    local_rows = block_rows % row_span
    local_cols = block_cols - dp_index * col_span
    row_pick = (local_rows[:, None] == jnp.arange(row_span, dtype=jnp.int32)[None, :]).astype(
        jnp.float32
    )
    col_pick = (local_cols[:, None] == jnp.arange(col_span, dtype=jnp.int32)[None, :]).astype(
        jnp.float32
    )
    added = jnp.einsum(
        "bx,by,brc->xryc",
        row_pick,
        col_pick,
        delta_values.astype(jnp.float32),
        precision=lax.Precision.HIGHEST,
    )
    w_eff = (base_weight.astype(jnp.float32) + added.reshape(feat_dev, col_span * BS)).astype(
        jnp.bfloat16
    )
    full_grad = lax.all_gather(out_grad, "tensor", axis=1, tiled=True)
    summed = lax.dot_general(
        full_grad,
        lax.all_gather(w_eff, "dp", axis=1, tiled=True),
        (((1,), (1,)), ((), ())),
        preferred_element_type=jnp.float32,
    )
    in_grad = summed.astype(jnp.bfloat16)
    left_sel = jnp.take(attn_out.reshape(tok_rows, row_span, BS), local_rows, axis=1)
    right_sel = jnp.take(full_grad.reshape(tok_rows, all_cols, BS), block_cols, axis=1)
    partial_blocks = jnp.einsum(
        "tbr,tbc->brc", left_sel, right_sel, preferred_element_type=jnp.float32
    )
    order = jnp.arange(piece_len, dtype=jnp.int32)
    same = block_owner[:, None] == block_owner[None, :]
    earlier = order[:, None] > order[None, :]
    slot = jnp.sum((same & earlier).astype(jnp.int32), axis=1)
    target = block_owner * slot_cap + slot
    places = jnp.arange(dp_count * slot_cap, dtype=jnp.int32)
    picker = (target[:, None] == places[None, :]).astype(jnp.float32)
    packed = jnp.einsum("bs,brc->src", picker, partial_blocks, precision=lax.Precision.HIGHEST)
    packed = packed.reshape(dp_count, slot_cap, BS, BS)
    received = lax.all_to_all(packed, "dp", split_axis=0, concat_axis=0, tiled=True)
    owned = jnp.sum(received, axis=0)
    return (in_grad, owned[None])


def solution(mesh):
    placed = (
        P(("groups", "dp"), "tensor"),
        P(("groups", "dp"), "tensor"),
        P("tensor", "dp"),
        P("tensor", None, None),
        P("tensor"),
        P("tensor"),
        P("tensor"),
    )
    return jax.shard_map(
        per_device,
        mesh=mesh,
        in_specs=placed,
        out_specs=(P(("groups", "dp"), "tensor"), P(("groups", "tensor"), "dp", None, None)),
        check_vma=False,
    )
```

profile of v0, /device:TPU:0, one launch (start us, length us, event | category | flops | bytes accessed | tf_op | source)
XLA Modules:
  0.0 420.6 jit_solution(16356854778635153784)
XLA Ops:
  7.2 0.0 copy-start.3
  7.2 0.0 copy-start.2
  7.2 0.0 copy-start.1
  7.2 0.0 all-gather.5.cloned.1.call-start
  7.2 4.0 copy.37
  11.2 0.0 all-gather.5.cloned.1.call-update
  11.3 0.0 all-gather.3.cloned.1.call-start
  11.3 0.0 copy-done.3
  11.4 0.0 copy-done.2
  11.4 6.7 %convolution_bitcast_fusion = f32[16,128,16,128]{3,0,1,2:T(8,128)S(1)} fusion(bf16[32,128,128]{2,1,0:T(8,128)(2,1)S(1)} %copy-done.1, f32[32,16]{0,1:T(8,128)S(1)} %get-tuple-element.17, f32[32,16]{0,1:T(8,128)S(1)} %get-tuple-element.16), kind=kOutput, calls=%fused_computation.4 | convolution fusion | flops 1610620928 | bytes 17829888 | tf_op jit(solution)/shard_map/bx,by,brc->xryc/dot_general | solution.py:28
  18.1 16.2 %copy.36 = f32[16,128,16,128]{3,2,1,0:T(8,128)S(1)} copy(f32[16,128,16,128]{3,0,1,2:T(8,128)S(1)} %convolution_bitcast_fusion) | data formatting | bytes 33554432 | tf_op jit(solution)/shard_map/bx,by,brc->xryc/transpose | solution.py:28
  34.3 11.6 %fusion = bf16[2048,2048]{1,0:T(8,128)(2,1)} fusion(f32[256,8,16,128]{3,2,1,0:T(8,128)S(1)} %bitcast.34, bf16[2048,2048]{1,0:T(8,128)(2,1)} %param.9), kind=kLoop, calls=%fused_computation.3 | loop fusion | flops 12582912 | bytes 33554432 | tf_op jit(solution)/shard_map/convert_element_type | solution.py:35
  45.9 0.0 all-gather.3.cloned.1.call-update
  45.9 1.6 copy-done
  47.5 2.5 copy.38
  50.0 3.0 copy.39
  53.1 0.0 copy-start.4
  53.1 3.0 gather_fusion
  56.1 0.0 copy-done.4
  56.1 0.2 convert_reduce_fusion
  56.3 107.4 %all-gather.5.cloned.1.call-done = bf16[512,8192]{0,1:T(8,128)(2,1)} async-done(((bf16[512,2048]{0,1:T(8,128)(2,1)}), bf16[512,8192]{0,1:T(8,128)(2,1)}) %all-gather.5.cloned.1.call-update) | async-done | bytes 8388624 | tf_op jit(solution)/shard_map/all_gather | solution.py:38
  163.8 12.3 %copy.40 = bf16[512,64,128]{2,0,1:T(8,128)(2,1)} copy(bf16[512,64,128]{0,2,1:T(8,128)(2,1)} %bitcast.35) | data formatting | bytes 16777216 | tf_op jit(solution)/shard_map/reshape | solution.py:47
  176.1 8.7 %gather_fusion.1 = bf16[32,512,128]{2,1,0:T(8,128)(2,1)} fusion(bf16[512,64,128]{2,0,1:T(8,128)(2,1)} %copy.40, s32[1024]{0:T(1024)S(1)} %pad_clamp_fusion), kind=kCustom, calls=%fused_computation.1 | custom fusion | bytes 8388736 | tf_op jit(solution)/shard_map/jit(_take)/gather | solution.py:47
  184.7 7.5 %fusion.1 = f32[32,128,128]{2,1,0:T(8,128)S(1)} fusion(bf16[32,512,128]{2,1,0:T(8,128)(2,1)} %gather_fusion.1, bf16[32,512,128]{2,1,0:T(8,128)(2,1)} %gather_fusion, pred[32]{0:T(512)(128)(4,1)S(1)} %compare_and_fusion, pred[32]{0:T(512)(128)(4,1)S(1)} %get-tuple-element.12), kind=kOutput, calls=%fused_computation.5 | convolution fusion | flops 541065216 | bytes 10485824 | tf_op jit(solution)/shard_map/tbr,tbc->brc/dot_general | solution.py:48
  192.3 2.4 fusion.12
  194.7 0.1 copy.43
  194.9 51.0 %all_to_all.5 = f32[4,8,128,128]{3,1,2,0:T(8,128)S(1)} all-to-all(f32[4,8,128,128]{3,1,2,0:T(8,128)S(1)} %copy.43), channel_id=1, replica_groups=mesh['groups'=2,'dp'=4,'tensor'=4] {'dp'}, dimensions={0} | all-to-all | bytes 4194304 | tf_op jit(solution)/shard_map/all_to_all | solution.py:60
  245.8 0.1 reduce_sum.19
  246.0 0.9 copy.46
  246.9 140.7 %all-gather.3.cloned.1.call-done = bf16[2048,8192]{1,0:T(8,128)(2,1)} async-done(((bf16[2048,2048]{1,0:T(8,128)(2,1)}), bf16[2048,8192]{1,0:T(8,128)(2,1)}) %all-gather.3.cloned.1.call-update) | async-done | bytes 33554448 | tf_op jit(solution)/shard_map/all_gather | solution.py:41
  387.6 23.8 %fusion.8 = bf16[512,2048]{0,1:T(8,128)(2,1)S(1)} fusion(bf16[2048,8192]{1,0:T(8,128)(2,1)} %all-gather.3.cloned.1.call-done, bf16[512,8192]{0,1:T(8,128)(2,1)} %all-gather.5.cloned.1.call-done), kind=kOutput, calls=%fused_computation.13 | convolution fusion | flops 17180917760 | bytes 44040192 | tf_op jit(solution)/shard_map/dot_general | solution.py:39
  411.3 2.4 copy.45
  (10 shorter events, 0.1 us)
Async XLA Ops:
  7.2 4.2 copy-start.3
  7.2 4.2 copy-start.2
  7.2 4.2 %copy-start.1 = (bf16[32,128,128]{2,1,0:T(8,128)(2,1)S(1)}, bf16[32,128,128]{2,1,0:T(8,128)(2,1)}, u32[]{:S(2)}) copy-start(bf16[32,128,128]{2,1,0:T(8,128)(2,1)} %param.10) | copy-start | bytes 3145732
  7.2 156.6 %all-gather.5.cloned.1.call-start = ((), (), s32[]{:S(2)}) async-start(), calls=%async_computation.2 | async-start | bytes 10485760 | tf_op jit(solution)/shard_map/all_gather | solution.py:38
  11.3 376.3 %all-gather.3.cloned.1.call-start = ((), (), s32[]{:S(2)}) async-start(), calls=%async_computation.1 | async-start | bytes 41943040 | tf_op jit(solution)/shard_map/all_gather | solution.py:41
  45.9 1.6 copy-start
  53.1 3.0 copy-start.4
Sparse Core Ops, SparseCore 0:
  11.4 152.3 all-gather.4
  165.3 222.2 all-gather.2
where the time goes:
time: 421 us
  waiting for transfers between devices  248 us (59%)
  local copies, waits for them, and re-layouts  54.7 us (13%)
  blocking collectives  51 us (12%)
  matrix products  40.4 us (10%)
  between operations  14.2 us (3%)
  other arithmetic  12 us (3%)
    all_gather x1, waiting for transfers between devices, per_device(): lax.all_gather(w_eff, 'dp', axis=1, tiled=True)  141 us
    all_gather x1, waiting for transfers between devices, per_device(): full_grad = lax.all_gather(out_grad, 'tensor', axis=1, tiled=True)  107 us
    all_to_all x1, blocking collectives, per_device(): lax.all_to_all(packed, 'dp', split_axis=0, concat_axis=0, tiled=True)  51 us
    dot_general x1, matrix products, per_device(): lax.dot_general(full_grad, lax.all_gather(w_eff, 'dp', axis=1, tiled=True...  23.8 us
    transpose x1, local copies, waits for them, and re-layouts, per_device(): jnp.einsum('bx,by,brc->xryc', row_pick, col_pick, delta_values.astype(jnp...  16.2 us
    reshape x1, local copies, waits for them, and re-layouts, per_device(): full_grad.reshape(tok_rows, all_cols, BS)  12.3 us
    convert_element_type x1, other arithmetic, per_device(): (base_weight.astype(jnp.float32) + added.reshape(feat_dev, col_span * BS)...  11.6 us
    unnamed x14, local copies, waits for them, and re-layouts  11.4 us
  transfers between devices with their start and end apart: 2, of which 2 were waited for; matrix products, arithmetic and copies ran while one was open for 18% of the time, Pallas kernels for 0%

commit v1 on v0

--- a/solution.py
+++ b/solution.py
@@ -1,6 +1,8 @@
 import jax
 import jax.numpy as jnp
 from jax import lax
+from jax.experimental import pallas as pl
+from jax.experimental.pallas import tpu as pltpu
 from jax.sharding import PartitionSpec as P
 
 D = 8192
@@ -62,6 +64,360 @@
     return (in_grad, owned[None])
 
 
+def build_tables(block_rows, block_cols, block_owner, row_span, col_span, dp_index, dp_count, slot_cap):
+    piece_len = block_owner.shape[0]
+    order = jnp.arange(piece_len, dtype=jnp.int32)
+    local_rows = block_rows % row_span
+    local_cols = block_cols - dp_index * col_span
+    cell = jnp.where(
+        (local_cols >= 0) & (local_cols < col_span), local_rows * col_span + local_cols, -1
+    )
+    cells = jnp.arange(row_span * col_span, dtype=jnp.int32)
+    here = cell[None, :] == cells[:, None]
+    entry_at = jnp.sum(jnp.where(here, order[None, :], 0), axis=1, dtype=jnp.int32)
+    entry_on = jnp.sum(here.astype(jnp.float32), axis=1)
+    same = block_owner[:, None] == block_owner[None, :]
+    earlier = order[:, None] > order[None, :]
+    slot = jnp.sum((same & earlier).astype(jnp.int32), axis=1)
+    target = block_owner * slot_cap + slot
+    places = jnp.arange(dp_count * slot_cap, dtype=jnp.int32)
+    there = target[None, :] == places[:, None]
+    facts = jnp.stack([local_rows, block_cols])
+    placed = jnp.sum(jnp.where(there[None], facts[:, None, :], 0), axis=2, dtype=jnp.int32)
+    placed_on = jnp.sum(there.astype(jnp.float32), axis=1)
+    return entry_at, entry_on, placed, placed_on
+
+
+N_DP = 4
+N_T = 4
+SLOTS = 8
+TOK = 512
+WID = 2048
+SPAN = WID // BS
+GCH = 4
+GBLK = SPAN // GCH
+WCH = 8
+HALF = WCH // 2
+WROWS = WID // WCH
+NT = 256
+MESH_ID = pl.DeviceIdType.MESH
+
+
+def fused(
+    entry_ref, entry_on_ref, placed_ref, placed_on_ref, attn_hbm, grad_hbm, base_hbm, delta_hbm, out_hbm, dgrad_hbm,
+    w_all, g_all, acc, stage, attn, attn_t, delta, dsend, drecv,
+    g_send, g_recv, w_send, w_recv, d_send, d_recv, loc,
+):
+    grp = lax.axis_index("groups")
+    me = lax.axis_index("dp")
+    t = lax.axis_index("tensor")
+    core = me % 2
+    mate = me + 1 - 2 * core
+    far = (me + 2) % 4
+    far_mate = (mate + 2) % 4
+
+    barrier = pltpu.get_barrier_semaphore()
+    for step in (1, 2, 3):
+        pl.semaphore_signal(
+            barrier, inc=1, device_id={"dp": (me + step) % 4}, device_id_type=MESH_ID
+        )
+    pl.semaphore_signal(barrier, inc=1, device_id={"groups": 1 - grp}, device_id_type=MESH_ID)
+
+    @pl.when(t > 0)
+    def _():
+        pl.semaphore_signal(barrier, inc=1, device_id={"tensor": t - 1}, device_id_type=MESH_ID)
+
+    @pl.when(t < N_T - 1)
+    def _():
+        pl.semaphore_signal(barrier, inc=1, device_id={"tensor": t + 1}, device_id_type=MESH_ID)
+
+    def base_copy(ch):
+        rows = pl.ds(pl.multiple_of(ch * WROWS, WROWS), WROWS)
+        return pltpu.make_async_copy(base_hbm.at[rows], w_all.at[me, rows], loc.at[ch])
+
+    def own_grad(b):
+        cols = pl.ds(b * BS, BS)
+        return pltpu.make_async_copy(
+            grad_hbm.at[:, cols], g_all.at[t * SPAN + b], loc.at[WCH + 3 + b]
+        )
+
+    attn_copy = pltpu.make_async_copy(attn_hbm, attn, loc.at[WCH + 1])
+    delta_copy = pltpu.make_async_copy(delta_hbm, delta, loc.at[WCH + 2])
+    for b in range(SPAN):
+        own_grad(b).start()
+    delta_copy.start()
+    for i in range(WCH):
+        base_copy((HALF * grp + i) % WCH).start()
+    attn_copy.start()
+
+    last = N_T - 1
+    pl.semaphore_wait(barrier, 4 + (t + last - 1) // last + (2 * last - 1 - t) // last)
+
+    def g_copy(shard, ch, side):
+        part = g_all.at[pl.ds(shard * SPAN + ch * GBLK, GBLK)]
+        return pltpu.make_async_remote_copy(
+            src_ref=part,
+            dst_ref=part,
+            send_sem=g_send.at[side, shard, ch],
+            recv_sem=g_recv.at[shard, ch],
+            device_id={"tensor": t - 1 if side == 0 else t + 1},
+            device_id_type=MESH_ID,
+        )
+
+    for ch in range(GCH):
+        for b in range(GBLK):
+            own_grad(ch * GBLK + b).wait()
+
+        @pl.when(t > 0)
+        def _():
+            g_copy(t, ch, 0).start()
+
+        @pl.when(t < N_T - 1)
+        def _():
+            g_copy(t, ch, 1).start()
+
+    X, Y, C_OWN, C_FAR = 0, 1, 2, 3
+
+    def w_copy(shard, ch, kind):
+        rows = pl.ds(pl.multiple_of(ch * WROWS, WROWS), WROWS)
+        if kind == X:
+            dev = {"dp": far}
+        elif kind == Y:
+            dev = {"groups": 1 - grp}
+        else:
+            dev = {"dp": mate}
+        return pltpu.make_async_remote_copy(
+            src_ref=w_all.at[shard, rows],
+            dst_ref=w_all.at[shard, rows],
+            send_sem=w_send.at[kind, ch],
+            recv_sem=w_recv.at[shard, ch],
+            device_id=dev,
+            device_id_type=MESH_ID,
+        )
+
+    delta_copy.wait()
+    for i in range(WCH):
+        ch = (HALF * grp + i) % WCH
+        base_copy(ch).wait()
+
+        def add_cell(n, carry, ch=ch):
+            r, c = n // SPAN, n % SPAN
+            rows = pl.ds(pl.multiple_of(ch * WROWS + r * BS, BS), BS)
+            cols = pl.ds(pl.multiple_of(c * BS, BS), BS)
+            at = ch * (WROWS // BS * SPAN) + n
+            extra = delta[entry_ref[at]].astype(jnp.float32) * entry_on_ref[at]
+            w_all[me, rows, cols] = (w_all[me, rows, cols].astype(jnp.float32) + extra).astype(
+                jnp.bfloat16
+            )
+            return carry
+
+        lax.fori_loop(0, WROWS // BS * SPAN, add_cell, 0)
+        if i < HALF:
+            w_copy(me, ch, X).start()
+        w_copy(me, ch, C_OWN).start()
+
+    attn_copy.wait()
+
+    def flip(r, carry):
+        cols = pl.ds(pl.multiple_of(r * BS, BS), BS)
+        attn_t[r] = attn[:, cols].T
+        return carry
+
+    lax.fori_loop(0, SPAN, flip, 0)
+
+    def left_in(m):
+        return t - 1 - m // GCH, m % GCH
+
+    def right_in(m):
+        return t + 1 + m // GCH, m % GCH
+
+    def take_left(m):
+        shard, ch = left_in(m)
+
+        @pl.when(shard >= 0)
+        def _():
+            g_copy(shard, ch, 1).wait_recv()
+
+            @pl.when(t < N_T - 1)
+            def _():
+                g_copy(shard, ch, 1).start()
+
+    def take_right(m):
+        shard, ch = right_in(m)
+
+        @pl.when(shard < N_T)
+        def _():
+            g_copy(shard, ch, 0).wait_recv()
+
+            @pl.when(t > 0)
+            def _():
+                g_copy(shard, ch, 0).start()
+
+    def x_in(i):
+        return HALF * grp + i
+
+    def y_in(i):
+        return HALF * (1 - grp) + i
+
+    for r in range(5):
+        if r < 4:
+            for m in (2 * r, 2 * r + 1):
+                take_left(m)
+                take_right(m)
+            w_copy(far, x_in(r), X).wait_recv()
+            w_copy(far, x_in(r), Y).start()
+            w_copy(far, x_in(r), C_FAR).start()
+        if r >= 1:
+            w_copy(far, y_in(r - 1), Y).wait_recv()
+            w_copy(far, y_in(r - 1), C_FAR).start()
+
+    for ch in range(WCH):
+        w_copy(mate, ch, C_OWN).wait_recv()
+    for ch in range(WCH):
+        w_copy(far_mate, ch, C_FAR).wait_recv()
+
+    def multiply(shard, first, last):
+        def tile(n, carry):
+            cols = pl.ds(pl.multiple_of(n * NT, NT), NT)
+            left = jnp.concatenate([g_all[shard * SPAN + b] for b in range(SPAN)], axis=1)
+            part = lax.dot_general(
+                left, w_all[shard, cols, :], (((1,), (1,)), ((), ())),
+                preferred_element_type=jnp.float32,
+            )
+            if first:
+                acc[:, cols] = part
+            elif last:
+                stage[:, cols] = (acc[:, cols] + part).astype(jnp.bfloat16)
+            else:
+                acc[:, cols] += part
+            return carry
+
+        lax.fori_loop(0, WID // NT, tile, 0)
+
+    away = jnp.where(t < N_T // 2, N_T - 1, 0)
+    toward = jnp.where(t < N_T // 2, 1, -1)
+    multiply((away + toward) % N_T, True, False)
+    multiply((away + 2 * toward) % N_T, False, False)
+    multiply((away + 3 * toward) % N_T, False, False)
+    for m in range(2 * GCH, 3 * GCH):
+        take_left(m)
+        take_right(m)
+
+    def one_place(p, carry):
+        block = jnp.dot(
+            attn_t[placed_ref[0, p]], g_all[placed_ref[1, p]],
+            preferred_element_type=jnp.float32,
+        )
+        dsend[p] = block * placed_on_ref[p]
+        return carry
+
+    def d_copy(peer):
+        return pltpu.make_async_remote_copy(
+            src_ref=dsend.at[pl.ds(pl.multiple_of(peer * SLOTS, SLOTS), SLOTS)],
+            dst_ref=drecv.at[me],
+            send_sem=d_send.at[peer],
+            recv_sem=d_recv.at[me],
+            device_id={"dp": peer},
+            device_id_type=MESH_ID,
+        )
+
+    def d_wait(peer):
+        return pltpu.make_async_remote_copy(
+            src_ref=dsend.at[pl.ds(pl.multiple_of(peer * SLOTS, SLOTS), SLOTS)],
+            dst_ref=drecv.at[peer],
+            send_sem=d_send.at[peer],
+            recv_sem=d_recv.at[peer],
+            device_id={"dp": peer},
+            device_id_type=MESH_ID,
+        )
+
+    for peer in (far, far_mate, mate):
+        lax.fori_loop(peer * SLOTS, (peer + 1) * SLOTS, one_place, 0)
+        d_copy(peer).start()
+    lax.fori_loop(me * SLOTS, (me + 1) * SLOTS, one_place, 0)
+
+    multiply(away, False, True)
+    out_copy = pltpu.make_async_copy(stage, out_hbm, loc.at[WCH + 3 + SPAN])
+    out_copy.start()
+
+    for peer in (mate, far, far_mate):
+        d_wait(peer).wait_recv()
+
+    def add_up(s, carry):
+        drecv[me, s] = (
+            dsend[me * SLOTS + s] + drecv[mate, s] + drecv[far, s] + drecv[far_mate, s]
+        )
+        return carry
+
+    lax.fori_loop(0, SLOTS, add_up, 0)
+    d_out = pltpu.make_async_copy(drecv.at[me], dgrad_hbm.at[0], loc.at[WCH + 4 + SPAN])
+    d_out.start()
+
+    for peer in (mate, far, far_mate):
+        d_copy(peer).wait_send()
+    for i in range(HALF):
+        w_copy(me, HALF * grp + i, X).wait_send()
+        w_copy(far, x_in(i), Y).wait_send()
+    for ch in range(WCH):
+        w_copy(me, ch, C_OWN).wait_send()
+        w_copy(far, ch, C_FAR).wait_send()
+    for shard in range(N_T):
+        for ch in range(GCH):
+            @pl.when((t > 0) & (shard >= t))
+            def _():
+                g_copy(shard, ch, 0).wait_send()
+
+            @pl.when((t < N_T - 1) & (shard <= t))
+            def _():
+                g_copy(shard, ch, 1).wait_send()
+    out_copy.wait()
+    d_out.wait()
+
+
+def per_device_fused(
+    attn_out, out_grad, base_weight, delta_values, block_rows, block_cols, block_owner
+):
+    tables = build_tables(
+        block_rows, block_cols, block_owner, SPAN, SPAN, lax.axis_index("dp"), N_DP, SLOTS
+    )
+    smem = pl.BlockSpec(memory_space=pltpu.SMEM)
+    hbm = pl.BlockSpec(memory_space=pl.ANY)
+    dma = pltpu.SemaphoreType.DMA
+    return tuple(pl.pallas_call(
+        fused,
+        out_shape=(
+            jax.ShapeDtypeStruct((TOK, WID), jnp.bfloat16),
+            jax.ShapeDtypeStruct((1, SLOTS, BS, BS), jnp.float32),
+        ),
+        in_specs=[smem, smem, smem, smem, hbm, hbm, hbm, hbm],
+        out_specs=(hbm, hbm),
+        scratch_shapes=[
+            pltpu.VMEM((N_DP, WID, WID), jnp.bfloat16),
+            pltpu.VMEM((N_T * SPAN, TOK, BS), jnp.bfloat16),
+            pltpu.VMEM((TOK, WID), jnp.float32),
+            pltpu.VMEM((TOK, WID), jnp.bfloat16),
+            pltpu.VMEM((TOK, WID), jnp.bfloat16),
+            pltpu.VMEM((SPAN, BS, TOK), jnp.bfloat16),
+            pltpu.VMEM((N_DP * SLOTS, BS, BS), jnp.bfloat16),
+            pltpu.VMEM((N_DP * SLOTS, BS, BS), jnp.float32),
+            pltpu.VMEM((N_DP, SLOTS, BS, BS), jnp.float32),
+            dma((2, N_T, GCH)),
+            dma((N_T, GCH)),
+            dma((4, WCH)),
+            dma((N_DP, WCH)),
+            dma((N_DP,)),
+            dma((N_DP,)),
+            dma((WCH + 5 + SPAN,)),
+        ],
+        compiler_params=pltpu.CompilerParams(
+            collective_id=0, has_side_effects=True, vmem_limit_bytes=60 * 1024 * 1024
+        ),
+        cost_estimate=pl.CostEstimate(
+            flops=2 * TOK * WID * D, bytes_accessed=16 * 1024 * 1024, transcendentals=0
+        ),
+    )(*tables, attn_out, out_grad, base_weight, delta_values))
+
+
 def solution(mesh):
     placed = (
         P(("groups", "dp"), "tensor"),
@@ -72,8 +428,9 @@
         P("tensor"),
         P("tensor"),
     )
+    here = (mesh.shape["groups"], mesh.shape["dp"], mesh.shape["tensor"])
     return jax.shard_map(
-        per_device,
+        per_device_fused if here == (2, N_DP, N_T) else per_device,
         mesh=mesh,
         in_specs=placed,
         out_specs=(P(("groups", "dp"), "tensor"), P(("groups", "tensor"), "dp", None, None)),

time: 421 us -> 180 us (0.43)
  waiting for transfers between devices: 248 us -> 0 us
  Pallas kernels: 0 us -> 169 us
  blocking collectives: 51 us -> 0 us
  local copies, waits for them, and re-layouts: 54.7 us -> 4.01 us
  matrix products: 40.4 us -> 0 us
  between operations: 14.2 us -> 0.66 us
  other arithmetic: 12 us -> 5.61 us
    all_gather x2 -> x0, waiting for transfers between devices: 248 us -> none  [the longest x1 141 us: per_device(): lax.all_gather(w_eff, 'dp', axis=1, tiled=True)]
    pallas_call x0 -> x1, Pallas kernels: none -> 169 us  [per_device_fused(): pl.pallas_call(fused, out_shape=(jax.ShapeDtypeStruct((TOK, WID), jnp.bfl...]
    all_to_all x1 -> x0, blocking collectives: 51 us -> none  [per_device(): lax.all_to_all(packed, 'dp', split_axis=0, concat_axis=0, tiled=True)]
    dot_general x4 -> x0, matrix products: 40.4 us -> none  [the longest x1 23.8 us: per_device(): lax.dot_general(full_grad, lax.all_gather(w_eff, 'dp', axis=1, tiled=True...]
    transpose x1 -> x0, local copies, waits for them, and re-layouts: 16.2 us -> none  [per_device(): jnp.einsum('bx,by,brc->xryc', row_pick, col_pick, delta_values.astype(jnp...]
    reshape x3 -> x0, local copies, waits for them, and re-layouts: 15.5 us -> none  [the longest x1 12.3 us: per_device(): full_grad.reshape(tok_rows, all_cols, BS)]
    gather x2 -> x0, local copies, waits for them, and re-layouts: 11.7 us -> none  [the longest x1 8.66 us: per_device(): jnp.take(full_grad.reshape(tok_rows, all_cols, BS), block_cols, axis=1)]
    convert_element_type x1 -> x0, other arithmetic: 11.6 us -> none  [per_device(): (base_weight.astype(jnp.float32) + added.reshape(feat_dev, col_span * BS)...]
  transfers between devices with their start and end apart: 2 -> 0, of which waited for: 2 -> 0; matrix products, arithmetic and copies ran while one was open for 18% -> 0% of each run, Pallas kernels for 0% -> 0%
where the time goes in v1:
time: 180 us
  Pallas kernels  169 us (94%)
  other arithmetic  5.61 us (3%)
  local copies, waits for them, and re-layouts  4.01 us (2%)
    pallas_call x1, Pallas kernels, per_device_fused(): pl.pallas_call(fused, out_shape=(jax.ShapeDtypeStruct((TOK, WID), jnp.bfl...  169 us
    unnamed x4, local copies, waits for them, and re-layouts  4.01 us

profile of v1, /device:TPU:0, one launch (start us, length us, event | category | flops | bytes accessed | tf_op | source)
XLA Modules:
  0.0 179.7 jit_solution(17292753329575232451)
XLA Ops:
  0.6 0.9 convert_reduce_fusion.2
  1.5 0.7 multiply_add_fusion
  2.2 0.7 convert_reduce_fusion.1.placed_on_ref
  2.9 0.7 and_select_fusion.1
  3.6 0.7 pad_add_fusion
  4.3 0.6 convert_reduce_fusion.entry_on_ref
  4.9 0.6 select_reduce_fusion.1.entry_ref
  5.6 0.7 select_reduce_fusion.placed_ref
  6.3 169.5 %shard_map.86 = (bf16[512,2048]{1,0:T(8,128)(2,1)}, f32[1,8,128,128]{3,2,1,0:T(8,128)}) custom-call(s32[256]{0:T(256)} %select_reduce_fusion.1.entry_ref, f32[256]{0:T(256)} %convert_reduce_fusion.entry_on_ref, s32[2,32]{1,0:T(2,128)} %select_reduce_fusion.placed_ref, f32[32]{0:T(128)} %convert_reduce_fusion.1.placed_on_ref, bf16[512,2048]{1,0:T(8,128)(2,1)} %attn_hbm.1, ...), custom_call_target="tpu_custom_call" | custom-call | flops 17179869184 | bytes 16777216 | tf_op jit(solution)/shard_map/pallas_call | solution.py:386
  175.7 0.0 copy-start
  175.7 3.2 %copy.11 = bf16[512,2048]{1,0:T(8,128)(2,1)} copy(bf16[512,2048]{1,0:T(8,128)(2,1)} %get-tuple-element.6) | data formatting | bytes 4194304
  178.9 0.0 copy-done
  178.9 0.8 copy.12
  (1 shorter events, 0.0 us)
Async XLA Ops:
  175.7 3.2 %copy-start = (f32[1,8,128,128]{3,2,1,0:T(8,128)S(1)}, f32[1,8,128,128]{3,2,1,0:T(8,128)}, u32[]{:S(2)}) copy-start(f32[1,8,128,128]{3,2,1,0:T(8,128)} %get-tuple-element.7) | copy-start | bytes 1572868

commit v2 on v1

--- a/solution.py
+++ b/solution.py
@@ -64,30 +64,6 @@
     return (in_grad, owned[None])
 
 
-def build_tables(block_rows, block_cols, block_owner, row_span, col_span, dp_index, dp_count, slot_cap):
-    piece_len = block_owner.shape[0]
-    order = jnp.arange(piece_len, dtype=jnp.int32)
-    local_rows = block_rows % row_span
-    local_cols = block_cols - dp_index * col_span
-    cell = jnp.where(
-        (local_cols >= 0) & (local_cols < col_span), local_rows * col_span + local_cols, -1
-    )
-    cells = jnp.arange(row_span * col_span, dtype=jnp.int32)
-    here = cell[None, :] == cells[:, None]
-    entry_at = jnp.sum(jnp.where(here, order[None, :], 0), axis=1, dtype=jnp.int32)
-    entry_on = jnp.sum(here.astype(jnp.float32), axis=1)
-    same = block_owner[:, None] == block_owner[None, :]
-    earlier = order[:, None] > order[None, :]
-    slot = jnp.sum((same & earlier).astype(jnp.int32), axis=1)
-    target = block_owner * slot_cap + slot
-    places = jnp.arange(dp_count * slot_cap, dtype=jnp.int32)
-    there = target[None, :] == places[:, None]
-    facts = jnp.stack([local_rows, block_cols])
-    placed = jnp.sum(jnp.where(there[None], facts[:, None, :], 0), axis=2, dtype=jnp.int32)
-    placed_on = jnp.sum(there.astype(jnp.float32), axis=1)
-    return entry_at, entry_on, placed, placed_on
-
-
 N_DP = 4
 N_T = 4
 SLOTS = 8
@@ -104,8 +80,9 @@
 
 
 def fused(
-    entry_ref, entry_on_ref, placed_ref, placed_on_ref, attn_hbm, grad_hbm, base_hbm, delta_hbm, out_hbm, dgrad_hbm,
-    w_all, g_all, acc, stage, attn, attn_t, delta, dsend, drecv,
+    rows_ref, cols_ref, owner_ref, attn_hbm, grad_hbm, base_hbm, delta_hbm, out_hbm, dgrad_hbm,
+    w_all, g_all, acc, stage, attn, attn_t, delta, dsend, core_in,
+    chip_sum, far_in, made, entry_ref, placed_ref,
     g_send, g_recv, w_send, w_recv, d_send, d_recv, loc,
 ):
     grp = lax.axis_index("groups")
@@ -117,10 +94,8 @@
     far_mate = (mate + 2) % 4
 
     barrier = pltpu.get_barrier_semaphore()
-    for step in (1, 2, 3):
-        pl.semaphore_signal(
-            barrier, inc=1, device_id={"dp": (me + step) % 4}, device_id_type=MESH_ID
-        )
+    for peer in (mate, far):
+        pl.semaphore_signal(barrier, inc=1, device_id={"dp": peer}, device_id_type=MESH_ID)
     pl.semaphore_signal(barrier, inc=1, device_id={"groups": 1 - grp}, device_id_type=MESH_ID)
 
     @pl.when(t > 0)
@@ -151,7 +126,7 @@
     attn_copy.start()
 
     last = N_T - 1
-    pl.semaphore_wait(barrier, 4 + (t + last - 1) // last + (2 * last - 1 - t) // last)
+    pl.semaphore_wait(barrier, 3 + (t + last - 1) // last + (2 * last - 1 - t) // last)
 
     def g_copy(shard, ch, side):
         part = g_all.at[pl.ds(shard * SPAN + ch * GBLK, GBLK)]
@@ -195,6 +170,32 @@
             device_id_type=MESH_ID,
         )
 
+    cell_row = lax.broadcasted_iota(jnp.int32, (SPAN, BS), 0)
+    cell_col = lax.broadcasted_iota(jnp.int32, (SPAN, BS), 1) + me * SPAN
+    place = lax.broadcasted_iota(jnp.int32, (SPAN, BS), 1)
+    place_owner, place_slot = place >> 3, place & (SLOTS - 1)
+    zero = jnp.zeros((SPAN, BS), jnp.int32)
+    entry, entry_on, seen, row_at, col_at, on_at = zero, zero, zero, zero, zero, zero
+    for n in range(rows_ref.shape[0]):
+        row, col, owner = rows_ref[n] & (SPAN - 1), cols_ref[n], owner_ref[n]
+        hit = (cell_row == row) & (cell_col == col)
+        entry = jnp.where(hit, n, entry)
+        entry_on = jnp.where(hit, 1, entry_on)
+        mine = place_owner == owner
+        fits = mine & (place_slot == seen)
+        row_at = jnp.where(fits, row, row_at)
+        col_at = jnp.where(fits, col, col_at)
+        on_at = jnp.where(fits, 1, on_at)
+        seen = jnp.where(mine, seen + 1, seen)
+    for n, table in enumerate((entry, entry_on, row_at, col_at, on_at)):
+        made[n] = table
+    entry_copy = pltpu.make_async_copy(made.at[pl.ds(0, 2)], entry_ref, loc.at[WCH + 5 + SPAN])
+    placed_copy = pltpu.make_async_copy(made.at[pl.ds(2, 3)], placed_ref, loc.at[WCH + 6 + SPAN])
+    entry_copy.start()
+    placed_copy.start()
+    entry_copy.wait()
+    placed_copy.wait()
+
     delta_copy.wait()
     for i in range(WCH):
         ch = (HALF * grp + i) % WCH
@@ -204,8 +205,9 @@
             r, c = n // SPAN, n % SPAN
             rows = pl.ds(pl.multiple_of(ch * WROWS + r * BS, BS), BS)
             cols = pl.ds(pl.multiple_of(c * BS, BS), BS)
-            at = ch * (WROWS // BS * SPAN) + n
-            extra = delta[entry_ref[at]].astype(jnp.float32) * entry_on_ref[at]
+            at = ch * (WROWS // BS) + r
+            extra = delta[entry_ref[0, at, c]].astype(jnp.float32)
+            extra = extra * entry_ref[1, at, c].astype(jnp.float32)
             w_all[me, rows, cols] = (w_all[me, rows, cols].astype(jnp.float32) + extra).astype(
                 jnp.bfloat16
             )
@@ -303,58 +305,77 @@
         take_left(m)
         take_right(m)
 
-    def one_place(p, carry):
-        block = jnp.dot(
-            attn_t[placed_ref[0, p]], g_all[placed_ref[1, p]],
-            preferred_element_type=jnp.float32,
-        )
-        dsend[p] = block * placed_on_ref[p]
-        return carry
-
-    def d_copy(peer):
+    def fill(peer):
+        def one_place(n, carry):
+            p = peer * SLOTS + n
+            block = jnp.dot(
+                attn_t[placed_ref[0, 0, p]], g_all[placed_ref[1, 0, p]],
+                preferred_element_type=jnp.float32,
+            )
+            dsend[p] = block * placed_ref[2, 0, p].astype(jnp.float32)
+            return carry
+
+        lax.fori_loop(0, SLOTS, one_place, 0, unroll=4)
+
+    def slots_of(peer):
+        return pl.ds(pl.multiple_of(peer * SLOTS, SLOTS), SLOTS)
+
+    def core_copy(side):
         return pltpu.make_async_remote_copy(
-            src_ref=dsend.at[pl.ds(pl.multiple_of(peer * SLOTS, SLOTS), SLOTS)],
-            dst_ref=drecv.at[me],
-            send_sem=d_send.at[peer],
-            recv_sem=d_recv.at[me],
-            device_id={"dp": peer},
+            src_ref=dsend.at[slots_of(far_mate if side == 0 else mate)],
+            dst_ref=core_in.at[side],
+            send_sem=d_send.at[side],
+            recv_sem=d_recv.at[side],
+            device_id={"dp": mate},
             device_id_type=MESH_ID,
         )
 
-    def d_wait(peer):
+    def far_copy():
         return pltpu.make_async_remote_copy(
-            src_ref=dsend.at[pl.ds(pl.multiple_of(peer * SLOTS, SLOTS), SLOTS)],
-            dst_ref=drecv.at[peer],
-            send_sem=d_send.at[peer],
-            recv_sem=d_recv.at[peer],
-            device_id={"dp": peer},
+            src_ref=chip_sum,
+            dst_ref=far_in,
+            send_sem=d_send.at[2],
+            recv_sem=d_recv.at[2],
+            device_id={"dp": far},
             device_id_type=MESH_ID,
         )
 
-    for peer in (far, far_mate, mate):
-        lax.fori_loop(peer * SLOTS, (peer + 1) * SLOTS, one_place, 0)
-        d_copy(peer).start()
-    lax.fori_loop(me * SLOTS, (me + 1) * SLOTS, one_place, 0)
+    fill(far_mate)
+    core_copy(0).start()
+    fill(far)
+    core_copy(0).wait_recv()
+
+    def chip_add(n, carry):
+        chip_sum[n] = (dsend[far * SLOTS + n] + core_in[0, n]).astype(jnp.bfloat16)
+        return carry
+
+    lax.fori_loop(0, SLOTS, chip_add, 0)
+    far_copy().start()
+    fill(mate)
+    core_copy(1).start()
+    fill(me)
 
     multiply(away, False, True)
     out_copy = pltpu.make_async_copy(stage, out_hbm, loc.at[WCH + 3 + SPAN])
     out_copy.start()
 
-    for peer in (mate, far, far_mate):
-        d_wait(peer).wait_recv()
-
-    def add_up(s, carry):
-        drecv[me, s] = (
-            dsend[me * SLOTS + s] + drecv[mate, s] + drecv[far, s] + drecv[far_mate, s]
-        )
+    core_copy(1).wait_recv()
+    far_copy().wait_recv()
+
+    def add_up(n, carry):
+        p = me * SLOTS + n
+        dsend[p] = dsend[p] + core_in[1, n] + far_in[n].astype(jnp.float32)
         return carry
 
     lax.fori_loop(0, SLOTS, add_up, 0)
-    d_out = pltpu.make_async_copy(drecv.at[me], dgrad_hbm.at[0], loc.at[WCH + 4 + SPAN])
+    d_out = pltpu.make_async_copy(
+        dsend.at[slots_of(me)], dgrad_hbm.at[0], loc.at[WCH + 4 + SPAN]
+    )
     d_out.start()
 
-    for peer in (mate, far, far_mate):
-        d_copy(peer).wait_send()
+    core_copy(0).wait_send()
+    core_copy(1).wait_send()
+    far_copy().wait_send()
     for i in range(HALF):
         w_copy(me, HALF * grp + i, X).wait_send()
         w_copy(far, x_in(i), Y).wait_send()
@@ -377,9 +398,6 @@
 def per_device_fused(
     attn_out, out_grad, base_weight, delta_values, block_rows, block_cols, block_owner
 ):
-    tables = build_tables(
-        block_rows, block_cols, block_owner, SPAN, SPAN, lax.axis_index("dp"), N_DP, SLOTS
-    )
     smem = pl.BlockSpec(memory_space=pltpu.SMEM)
     hbm = pl.BlockSpec(memory_space=pl.ANY)
     dma = pltpu.SemaphoreType.DMA
@@ -389,7 +407,7 @@
             jax.ShapeDtypeStruct((TOK, WID), jnp.bfloat16),
             jax.ShapeDtypeStruct((1, SLOTS, BS, BS), jnp.float32),
         ),
-        in_specs=[smem, smem, smem, smem, hbm, hbm, hbm, hbm],
+        in_specs=[smem, smem, smem, hbm, hbm, hbm, hbm],
         out_specs=(hbm, hbm),
         scratch_shapes=[
             pltpu.VMEM((N_DP, WID, WID), jnp.bfloat16),
@@ -400,14 +418,19 @@
             pltpu.VMEM((SPAN, BS, TOK), jnp.bfloat16),
             pltpu.VMEM((N_DP * SLOTS, BS, BS), jnp.bfloat16),
             pltpu.VMEM((N_DP * SLOTS, BS, BS), jnp.float32),
-            pltpu.VMEM((N_DP, SLOTS, BS, BS), jnp.float32),
+            pltpu.VMEM((2, SLOTS, BS, BS), jnp.float32),
+            pltpu.VMEM((SLOTS, BS, BS), jnp.bfloat16),
+            pltpu.VMEM((SLOTS, BS, BS), jnp.bfloat16),
+            pltpu.VMEM((5, SPAN, BS), jnp.int32),
+            pltpu.SMEM((2, SPAN, BS), jnp.int32),
+            pltpu.SMEM((3, SPAN, BS), jnp.int32),
             dma((2, N_T, GCH)),
             dma((N_T, GCH)),
             dma((4, WCH)),
             dma((N_DP, WCH)),
-            dma((N_DP,)),
-            dma((N_DP,)),
-            dma((WCH + 5 + SPAN,)),
+            dma((3,)),
+            dma((3,)),
+            dma((WCH + 7 + SPAN,)),
         ],
         compiler_params=pltpu.CompilerParams(
             collective_id=0, has_side_effects=True, vmem_limit_bytes=60 * 1024 * 1024
@@ -415,7 +438,9 @@
         cost_estimate=pl.CostEstimate(
             flops=2 * TOK * WID * D, bytes_accessed=16 * 1024 * 1024, transcendentals=0
         ),
-    )(*tables, attn_out, out_grad, base_weight, delta_values))
+    )(
+        block_rows, block_cols, block_owner, attn_out, out_grad, base_weight, delta_values
+    ))
 
 
 def solution(mesh):

time: 180 us -> 160 us (0.89)
  Pallas kernels: 169 us -> 155 us
  other arithmetic: 5.61 us -> 0 us
    pallas_call x1, Pallas kernels: 169 us -> 155 us  [per_device_fused(): pl.pallas_call(fused, out_shape=(jax.ShapeDtypeStruct((TOK, WID), jnp.bfl...]
    reduce_sum x5 -> x0, other arithmetic: 3.59 us -> none  [the longest x1 0.91 us: build_tables(): slot = jnp.sum((same & earlier).astype(jnp.int32), axis=1)]
where the time goes in v2:
time: 160 us
  Pallas kernels  155 us (97%)
  local copies, waits for them, and re-layouts  4.01 us (3%)
    pallas_call x1, Pallas kernels, per_device_fused(): pl.pallas_call(fused, out_shape=(jax.ShapeDtypeStruct((TOK, WID), jnp.bfl...  155 us
    unnamed x4, local copies, waits for them, and re-layouts  4.01 us

profile of v2, /device:TPU:0, one launch (start us, length us, event | category | flops | bytes accessed | tf_op | source)
XLA Modules:
  0.0 159.5 jit_solution(4936949461536092203)
XLA Ops:
  0.6 154.9 %shard_map.86 = (bf16[512,2048]{1,0:T(8,128)(2,1)}, f32[1,8,128,128]{3,2,1,0:T(8,128)}) custom-call(s32[32]{0:T(128)} %rows_ref.1, s32[32]{0:T(128)} %cols_ref.1, s32[32]{0:T(128)} %owner_ref.1, bf16[512,2048]{1,0:T(8,128)(2,1)} %attn_hbm.1, bf16[512,2048]{1,0:T(8,128)(2,1)} %grad_hbm.1, bf16[2048,2048]{1,0:T(8,128)(2,1)} %base_hbm.1, ...), custom_call_target="tpu_custom_call" | custom-call | flops 17179869184 | bytes 16777216 | tf_op jit(solution)/shard_map/pallas_call | solution.py:404
  155.5 0.0 copy-start
  155.5 3.2 %copy.11 = bf16[512,2048]{1,0:T(8,128)(2,1)} copy(bf16[512,2048]{1,0:T(8,128)(2,1)} %get-tuple-element.4) | data formatting | bytes 4194304
  158.8 0.0 copy-done
  158.8 0.8 copy.12
Async XLA Ops:
  155.5 3.2 %copy-start = (f32[1,8,128,128]{3,2,1,0:T(8,128)S(1)}, f32[1,8,128,128]{3,2,1,0:T(8,128)}, u32[]{:S(2)}) copy-start(f32[1,8,128,128]{3,2,1,0:T(8,128)} %get-tuple-element.5) | copy-start | bytes 1572868

commit v3 on v2

--- a/solution.py
+++ b/solution.py
@@ -80,8 +80,8 @@
 
 
 def fused(
-    rows_ref, cols_ref, owner_ref, attn_hbm, grad_hbm, base_hbm, delta_hbm, out_hbm, dgrad_hbm,
-    w_all, g_all, acc, stage, attn, attn_t, delta, dsend, core_in,
+    rows_ref, cols_ref, owner_ref, attn_hbm, grad_hbm, base_hbm, delta_hbm, out_ref, dgrad_ref,
+    w_all, g_all, acc, attn, attn_t, delta, dsend, core_in,
     chip_sum, far_in, made, entry_ref, placed_ref,
     g_send, g_recv, w_send, w_recv, d_send, d_recv, loc,
 ):
@@ -263,7 +263,7 @@
 
     for r in range(5):
         if r < 4:
-            for m in (2 * r, 2 * r + 1):
+            for m in range(r * GCH // 2, (r + 1) * GCH // 2):
                 take_left(m)
                 take_right(m)
             w_copy(far, x_in(r), X).wait_recv()
@@ -289,7 +289,7 @@
             if first:
                 acc[:, cols] = part
             elif last:
-                stage[:, cols] = (acc[:, cols] + part).astype(jnp.bfloat16)
+                out_ref[:, cols] = (acc[:, cols] + part).astype(jnp.bfloat16)
             else:
                 acc[:, cols] += part
             return carry
@@ -356,23 +356,16 @@
     fill(me)
 
     multiply(away, False, True)
-    out_copy = pltpu.make_async_copy(stage, out_hbm, loc.at[WCH + 3 + SPAN])
-    out_copy.start()
 
     core_copy(1).wait_recv()
     far_copy().wait_recv()
 
     def add_up(n, carry):
         p = me * SLOTS + n
-        dsend[p] = dsend[p] + core_in[1, n] + far_in[n].astype(jnp.float32)
+        dgrad_ref[0, n] = dsend[p] + core_in[1, n] + far_in[n].astype(jnp.float32)
         return carry
 
     lax.fori_loop(0, SLOTS, add_up, 0)
-    d_out = pltpu.make_async_copy(
-        dsend.at[slots_of(me)], dgrad_hbm.at[0], loc.at[WCH + 4 + SPAN]
-    )
-    d_out.start()
-
     core_copy(0).wait_send()
     core_copy(1).wait_send()
     far_copy().wait_send()
@@ -391,8 +384,6 @@
             @pl.when((t < N_T - 1) & (shard <= t))
             def _():
                 g_copy(shard, ch, 1).wait_send()
-    out_copy.wait()
-    d_out.wait()
 
 
 def per_device_fused(
@@ -404,16 +395,15 @@
     return tuple(pl.pallas_call(
         fused,
         out_shape=(
-            jax.ShapeDtypeStruct((TOK, WID), jnp.bfloat16),
-            jax.ShapeDtypeStruct((1, SLOTS, BS, BS), jnp.float32),
+            pltpu.VMEM((TOK, WID), jnp.bfloat16),
+            pltpu.VMEM((1, SLOTS, BS, BS), jnp.float32),
         ),
         in_specs=[smem, smem, smem, hbm, hbm, hbm, hbm],
-        out_specs=(hbm, hbm),
+        out_specs=(pl.BlockSpec(memory_space=pltpu.VMEM),) * 2,
         scratch_shapes=[
             pltpu.VMEM((N_DP, WID, WID), jnp.bfloat16),
             pltpu.VMEM((N_T * SPAN, TOK, BS), jnp.bfloat16),
             pltpu.VMEM((TOK, WID), jnp.float32),
-            pltpu.VMEM((TOK, WID), jnp.bfloat16),
             pltpu.VMEM((TOK, WID), jnp.bfloat16),
             pltpu.VMEM((SPAN, BS, TOK), jnp.bfloat16),
             pltpu.VMEM((N_DP * SLOTS, BS, BS), jnp.bfloat16),
@@ -433,7 +423,7 @@
             dma((WCH + 7 + SPAN,)),
         ],
         compiler_params=pltpu.CompilerParams(
-            collective_id=0, has_side_effects=True, vmem_limit_bytes=60 * 1024 * 1024
+            collective_id=0, has_side_effects=True, vmem_limit_bytes=58 * 1024 * 1024
         ),
         cost_estimate=pl.CostEstimate(
             flops=2 * TOK * WID * D, bytes_accessed=16 * 1024 * 1024, transcendentals=0

time: 160 us -> 156 us (0.975)
  local copies, waits for them, and re-layouts: 4.01 us -> 2.11 us
    unnamed x4 -> x2, local copies, waits for them, and re-layouts: 4.01 us -> 2.11 us
where the time goes in v3:
time: 156 us
  Pallas kernels  154 us (99%)
  local copies, waits for them, and re-layouts  2.11 us (1%)
    pallas_call x1, Pallas kernels, per_device_fused(): pl.pallas_call(fused, out_shape=(pltpu.VMEM((TOK, WID), jnp.bfloat16), pl...  154 us

profile of v3, /device:TPU:0, one launch (start us, length us, event | category | flops | bytes accessed | tf_op | source)
XLA Modules:
  0.0 156.3 jit_solution(2887582048232797463)
XLA Ops:
  0.6 153.5 %shard_map.86 = (bf16[512,2048]{1,0:T(8,128)(2,1)S(1)}, f32[1,8,128,128]{3,2,1,0:T(8,128)S(1)}) custom-call(s32[32]{0:T(128)} %rows_ref.1, s32[32]{0:T(128)} %cols_ref.1, s32[32]{0:T(128)} %owner_ref.1, bf16[512,2048]{1,0:T(8,128)(2,1)} %attn_hbm.1, bf16[512,2048]{1,0:T(8,128)(2,1)} %grad_hbm.1, bf16[2048,2048]{1,0:T(8,128)(2,1)} %base_hbm.1, ...), custom_call_target="tpu_custom_call" | custom-call | flops 17179869184 | bytes 16777216 | tf_op jit(solution)/shard_map/pallas_call | solution.py:395
  154.2 1.3 copy.11
  155.5 0.8 copy.12

commit v4 on v3

--- a/solution.py
+++ b/solution.py
@@ -75,7 +75,7 @@
 WCH = 8
 HALF = WCH // 2
 WROWS = WID // WCH
-NT = 256
+NT = 512
 MESH_ID = pl.DeviceIdType.MESH
 
 
@@ -315,7 +315,7 @@
             dsend[p] = block * placed_ref[2, 0, p].astype(jnp.float32)
             return carry
 
-        lax.fori_loop(0, SLOTS, one_place, 0, unroll=4)
+        lax.fori_loop(0, SLOTS, one_place, 0, unroll=8)
 
     def slots_of(peer):
         return pl.ds(pl.multiple_of(peer * SLOTS, SLOTS), SLOTS)

time: 156 us -> 154 us (0.987)
  Pallas kernels: 154 us -> 151 us
    pallas_call x1, Pallas kernels: 154 us -> 151 us  [per_device_fused(): pl.pallas_call(fused, out_shape=(pltpu.VMEM((TOK, WID), jnp.bfloat16), pl...]
where the time goes in v4:
time: 154 us
  Pallas kernels  151 us (98%)
  local copies, waits for them, and re-layouts  2.11 us (1%)
    pallas_call x1, Pallas kernels, per_device_fused(): pl.pallas_call(fused, out_shape=(pltpu.VMEM((TOK, WID), jnp.bfloat16), pl...  151 us

profile of v4, /device:TPU:0, one launch (start us, length us, event | category | flops | bytes accessed | tf_op | source)
XLA Modules:
  0.0 153.7 jit_solution(8258713375993123071)
XLA Ops:
  0.6 150.9 %shard_map.86 = (bf16[512,2048]{1,0:T(8,128)(2,1)S(1)}, f32[1,8,128,128]{3,2,1,0:T(8,128)S(1)}) custom-call(s32[32]{0:T(128)} %rows_ref.1, s32[32]{0:T(128)} %cols_ref.1, s32[32]{0:T(128)} %owner_ref.1, bf16[512,2048]{1,0:T(8,128)(2,1)} %attn_hbm.1, bf16[512,2048]{1,0:T(8,128)(2,1)} %grad_hbm.1, bf16[2048,2048]{1,0:T(8,128)(2,1)} %base_hbm.1, ...), custom_call_target="tpu_custom_call" | custom-call | flops 17179869184 | bytes 16777216 | tf_op jit(solution)/shard_map/pallas_call | solution.py:395
  151.5 1.3 copy.11
  152.9 0.8 copy.12
